TPU v7x, 32 devices: a whole 2x2x4 slice. The times are simulated.
32 devices in a mesh: groups: 2 (over y), space: 4 (over z), feat: 2 (over x), sub: 2 (over core).
Axes of the slice: x: 2, y: 2, z: 4, core: 2. Of those that a mesh axis runs over, the one named last changes fastest.
Arguments:
- x_grid: bfloat16 [2048, 227], P(('groups', 'space')), parts along dimension 0, may hold values from -6 to 6
- mesh_nodes: bfloat16 [1024, 512], P('space', 'feat'), may hold values from -6 to 6
- w_embed: bfloat16 [227, 512], P(None, 'feat'), may hold values from -0.375 to 0.375
- w_send: bfloat16 [3, 512, 512], P(None, None, 'feat'), may hold values from -0.25 to 0.25
- w_recv: bfloat16 [3, 512, 512], P(None, None, 'feat'), may hold values from -0.25 to 0.25
- w_out: bfloat16 [3, 512, 512], P(None, 'feat'), may hold values from -0.03125 to 0.03125
- edge_bias: float32 [3, 512], P(None, 'feat'), may hold values from -4 to 4
- enc_sources: int32 [128, 128], P(('space', 'sub')), may hold values from 0 to 255
- enc_owners: int32 [128, 1], P(('space', 'sub')), may hold values from 0 to 3; in each aligned block of 16 rows (0 to 15, 16 to 31, ...) at most 8 rows name the same one
- enc_blocks: int32 [128], P(('space', 'sub')), may hold values from 0 to 1
- enc_offsets: int32 [128, 128], P(('space', 'sub')), may hold values from -1 to 127
- proc_sources: int32 [128, 128], P(('space', 'sub')), may hold values from 0 to 255
- proc_owners: int32 [128, 1], P(('space', 'sub')), may hold values from 0 to 3; in each aligned block of 16 rows (0 to 15, 16 to 31, ...) at most 8 rows name the same one
- proc_blocks: int32 [128], P(('space', 'sub')), may hold values from 0 to 1
- proc_offsets: int32 [128, 128], P(('space', 'sub')), may hold values from -1 to 127
- dec_sources: int32 [128, 128], P(('space', 'sub')), may hold values from 0 to 255
- dec_owners: int32 [128, 1], P(('space', 'sub')), may hold values from 0 to 3; in each aligned block of 16 rows (0 to 15, 16 to 31, ...) at most 8 rows name the same one
- dec_blocks: int32 [128], P(('space', 'sub')), may hold values from 0 to 1
- dec_offsets: int32 [128, 128], P(('space', 'sub')), may hold values from -1 to 127
Outputs:
- grid_out: bfloat16 [2048, 512], P(('groups', 'space'), 'feat'), parts along dimension 0
There are 2 independent parts, one for each index of `groups`. A program takes and returns all parts, laid end to end along the dimension named above; an argument that names none is the same for every part. Nothing has to cross between parts.
Inputs may be any that keep to these rules, and one draw needn't show every extreme that they name: `enc_owners`: among the 16 edge blocks of one device, no owner is named more than 8 times, a bound that some block reaches. `proc_owners`: as for enc_owners. `dec_owners`: as for enc_owners.
All inputs are finite; a program needn't handle non-finite values.
Results may differ from a plain program's by a relative error of at most 0.0055.
Values may be sent and summed in bfloat16 or wider, within the bound.
A program may use at most 64 MiB of HBM per device.

v0:
```python
import jax
import jax.numpy as jnp
from jax import lax
from jax.sharding import PartitionSpec as P


def make_hidden(send_part, recv_part, offsets, bias_cols):
    value = send_part.astype(jnp.float32) + recv_part.astype(jnp.float32) + bias_cols
    hidden = jax.nn.silu(value)
    return jnp.where((offsets >= 0)[..., None], hidden, 0.0).astype(jnp.bfloat16)


def block_sum(hidden, offsets, block_ids, block_total):
    node_hot = (offsets[:, :, None] == jnp.arange(128, dtype=jnp.int32)[None, None, :]).astype(
        jnp.bfloat16
    )
    per_block = jnp.einsum("nep,nec->npc", node_hot, hidden, preferred_element_type=jnp.float32)
    block_hot = (block_ids[:, None] == jnp.arange(block_total, dtype=jnp.int32)[None, :]).astype(
        jnp.float32
    )
    summed = jnp.einsum("nb,npc->bpc", block_hot, per_block, precision=lax.Precision.HIGHEST)
    return summed.reshape(block_total * 128, hidden.shape[2])


def section(
    sender,
    receiver,
    section_index,
    w_send,
    w_recv,
    w_out,
    edge_bias,
    sources,
    owners,
    blocks,
    offsets,
):
    send_weight = w_send[section_index]
    recv_weight = w_recv[section_index]
    bias_cols = edge_bias[section_index]
    send_proj = jnp.dot(
        lax.all_gather(sender, "feat", axis=1, tiled=True),
        send_weight,
        preferred_element_type=jnp.float32,
    )
    recv_proj = jnp.dot(
        lax.all_gather(receiver, "feat", axis=1, tiled=True),
        recv_weight,
        preferred_element_type=jnp.float32,
    )
    send_proj = send_proj.astype(jnp.bfloat16)
    recv_proj = recv_proj.astype(jnp.bfloat16)
    recv_count = receiver.shape[0]
    recv_blocks = recv_count // 128
    owner_ids = owners[:, 0]
    space_count = lax.axis_size("space")
    block_count = sources.shape[0]
    capacity = max(2, 2 * block_count // space_count)
    slot_count = space_count * capacity
    owner_hot = (owner_ids[:, None] == jnp.arange(space_count, dtype=jnp.int32)[None, :]).astype(
        jnp.int32
    )
    place_rank = jnp.sum((jnp.cumsum(owner_hot, axis=0) - owner_hot) * owner_hot, axis=1)
    slot_of_block = owner_ids * capacity + place_rank
    slot_match = slot_of_block[None, :] == jnp.arange(slot_count, dtype=jnp.int32)[:, None]
    occupied = jnp.any(slot_match, axis=1)
    block_pick = jnp.sum(
        jnp.where(slot_match, jnp.arange(block_count, dtype=jnp.int32)[None, :], 0), axis=1
    )
    sent_offsets = jnp.where(occupied[:, None], offsets[block_pick], -1)
    sent_blocks = blocks[block_pick]
    send_rows = send_proj[sources[block_pick]]
    sent_data = jnp.where(occupied[:, None, None], send_rows, jnp.zeros_like(send_rows))
    arrived, arrived_offsets, arrived_blocks = (
        lax.all_to_all(sent_data, "space", split_axis=0, concat_axis=0, tiled=True),
        lax.all_to_all(sent_offsets, "space", split_axis=0, concat_axis=0, tiled=True),
        lax.all_to_all(sent_blocks, "space", split_axis=0, concat_axis=0, tiled=True),
    )
    target_rows = arrived_blocks[:, None] * 128 + jnp.maximum(arrived_offsets, 0)
    hidden = make_hidden(arrived, recv_proj[target_rows], arrived_offsets, bias_cols)
    edge_sums = block_sum(hidden, arrived_offsets, arrived_blocks, recv_blocks)
    edge_sums = lax.psum(edge_sums, "sub")
    out_rows = w_out[section_index].astype(jnp.float32)
    partial_update = jnp.dot(edge_sums, out_rows, precision=lax.Precision.HIGHEST)
    update = lax.psum_scatter(partial_update, "feat", scatter_dimension=1, tiled=True)
    return (receiver.astype(jnp.float32) + update).astype(jnp.bfloat16)


def on_device(
    x_grid,
    mesh_nodes,
    w_embed,
    w_send,
    w_recv,
    w_out,
    edge_bias,
    enc_sources,
    enc_owners,
    enc_blocks,
    enc_offsets,
    proc_sources,
    proc_owners,
    proc_blocks,
    proc_offsets,
    dec_sources,
    dec_owners,
    dec_blocks,
    dec_offsets,
):
    grid = jnp.dot(x_grid, w_embed, preferred_element_type=jnp.float32).astype(jnp.bfloat16)
    mesh_one = section(
        grid,
        mesh_nodes,
        0,
        w_send,
        w_recv,
        w_out,
        edge_bias,
        enc_sources,
        enc_owners,
        enc_blocks,
        enc_offsets,
    )
    mesh_two = section(
        mesh_one,
        mesh_one,
        1,
        w_send,
        w_recv,
        w_out,
        edge_bias,
        proc_sources,
        proc_owners,
        proc_blocks,
        proc_offsets,
    )
    return section(
        mesh_two,
        grid,
        2,
        w_send,
        w_recv,
        w_out,
        edge_bias,
        dec_sources,
        dec_owners,
        dec_blocks,
        dec_offsets,
    )


def solution(mesh):
    in_specs = (
        P(("groups", "space"), None),
        P("space", "feat"),
        P(None, "feat"),
        P(None, None, "feat"),
        P(None, None, "feat"),
        P(None, "feat", None),
        P(None, "feat"),
        P(("space", "sub"), None),
        P(("space", "sub"), None),
        P(("space", "sub")),
        P(("space", "sub"), None),
        P(("space", "sub"), None),
        P(("space", "sub"), None),
        P(("space", "sub")),
        P(("space", "sub"), None),
        P(("space", "sub"), None),
        P(("space", "sub"), None),
        P(("space", "sub")),
        P(("space", "sub"), None),
    )
    out_specs = P(("groups", "space"), "feat")
    return jax.shard_map(
        on_device, mesh=mesh, in_specs=in_specs, out_specs=out_specs, check_vma=False
    )
```

profile of v0, /device:TPU:1, one launch (start us, length us, event | category | flops | bytes accessed | tf_op | source)
XLA Modules:
  0.0 406.9 jit_solution(11922991904369965828)
XLA Ops:
  11.0 5.4 %all-to-all-start.2 = ((s32[4,8,1]{1,2,0:T(1,128)}), s32[4,8,1]{1,2,0:T(1,128)S(1)}, u32[]{:S(2)}, u32[]{:S(2)}) async-start(s32[4,8,1]{1,2,0:T(1,128)} %bitcast.10), calls=%async_computation.2 | async-start | bytes 4096 | tf_op jit(solution)/shard_map/all_to_all | solution.py:77
  20.3 4.5 %all_gather.14 = bf16[256,512]{1,0:T(8,128)(2,1)S(1)} all-gather(bf16[256,256]{1,0:T(8,128)(2,1)S(1)} %convolution_convert_fusion.6), channel_id=1, replica_groups=mesh['groups'=2,'space'=4,'feat'=2,'sub'=2] {'feat'}, dimensions={1}, use_global_device_ids=true | all-gather | bytes 393216 | tf_op jit(solution)/shard_map/all_gather | solution.py:42
  26.6 14.6 %gather_fusion.5 = bf16[4096,256]{1,0:T(8,128)(2,1)S(1)} fusion(bf16[256,256]{1,0:T(8,128)(2,1)S(1)} %convolution_convert_fusion.5, s32[4096]{0:T(1024)S(1)} %fusion.40), kind=kCustom, calls=%fused_computation.5 | custom fusion | bytes 4210688 | tf_op jit(solution)/shard_map/gather | solution.py:72
  41.3 4.5 %all-to-all-start.3 = ((s32[4,8,128]{2,1,0:T(8,128)}), s32[4,8,128]{2,1,0:T(8,128)S(1)}, u32[]{:S(2)}, u32[]{:S(2)}) async-start(s32[4,8,128]{2,1,0:T(8,128)} %bitcast_select_fusion.1), calls=%async_computation.3 | async-start | bytes 32768 | tf_op jit(solution)/shard_map/all_to_all | solution.py:76
  61.0 16.9 %gather_fusion.6 = bf16[4096,256]{1,0:T(8,128)(2,1)} fusion(bf16[256,256]{1,0:T(8,128)(2,1)S(1)} %convolution_convert_fusion.4, s32[4096]{0:T(1024)S(1)} %fusion.42), kind=kCustom, calls=%fused_computation.6 | custom fusion | bytes 4210688 | tf_op jit(solution)/shard_map/gather | solution.py:80
  77.9 23.6 %all-to-all-done.4 = bf16[32,128,256]{2,1,0:T(8,128)(2,1)S(1)} async-done(((bf16[32,128,256]{2,1,0:T(8,128)(2,1)}), bf16[32,128,256]{2,1,0:T(8,128)(2,1)S(1)}, u32[]{:S(2)}, u32[]{:S(2)}) %all-to-all-start.4) | async-done | bytes 2097184 | tf_op jit(solution)/shard_map/all_to_all | solution.py:75
  110.4 18.3 %all-reduce.4.cloned.1.call-done = f32[256,256]{1,0:T(8,128)} async-done(((f32[256,256]{1,0:T(8,128)}), f32[256,256]{1,0:T(8,128)}) %all-reduce.4.cloned.1.call-update) | async-done | bytes 262160 | tf_op jit(solution)/shard_map/psum | solution.py:82
  132.5 4.7 %all-to-all-start.5 = ((s32[4,8,1]{1,2,0:T(1,128)}), s32[4,8,1]{1,2,0:T(1,128)S(1)}, u32[]{:S(2)}, u32[]{:S(2)}) async-start(s32[4,8,1]{1,2,0:T(1,128)} %bitcast.28), calls=%async_computation.6 | async-start | bytes 4096 | tf_op jit(solution)/shard_map/all_to_all | solution.py:77
  139.2 7.3 %reduce-scatter.4.cloned.1.call-done = f32[256,256]{1,0:T(8,128)} async-done(((f32[256,512]{1,0:T(8,128)}), f32[256,256]{1,0:T(8,128)}) %reduce-scatter.4.cloned.1.call-update) | async-done | bytes 262160 | tf_op jit(solution)/shard_map/reduce_scatter | solution.py:85
  147.5 5.0 %all_gather.16 = bf16[256,512]{1,0:T(8,128)(2,1)S(1)} all-gather(bf16[256,256]{1,0:T(8,128)(2,1)S(1)} %add_convert_fusion.2), channel_id=1, replica_groups=mesh['groups'=2,'space'=4,'feat'=2,'sub'=2] {'feat'}, dimensions={1}, use_global_device_ids=true | all-gather | bytes 393216 | tf_op jit(solution)/shard_map/all_gather | solution.py:42
  153.7 14.6 %gather_fusion.10 = bf16[4096,256]{1,0:T(8,128)(2,1)S(1)} fusion(bf16[256,256]{1,0:T(8,128)(2,1)S(1)} %convolution_convert_fusion.3, s32[4096]{0:T(1024)S(1)} %fusion.44), kind=kCustom, calls=%fused_computation.10 | custom fusion | bytes 4210688 | tf_op jit(solution)/shard_map/gather | solution.py:72
  168.3 4.5 %all-to-all-start.6 = ((s32[4,8,128]{2,1,0:T(8,128)}), s32[4,8,128]{2,1,0:T(8,128)S(1)}, u32[]{:S(2)}, u32[]{:S(2)}) async-start(s32[4,8,128]{2,1,0:T(8,128)} %bitcast_select_fusion), calls=%async_computation.7 | async-start | bytes 32768 | tf_op jit(solution)/shard_map/all_to_all | solution.py:76
  183.1 16.9 %gather_fusion.11 = bf16[4096,256]{1,0:T(8,128)(2,1)} fusion(bf16[256,256]{1,0:T(8,128)(2,1)S(1)} %convolution_convert_fusion.2, s32[4096]{0:T(1024)S(1)} %fusion.46), kind=kCustom, calls=%fused_computation.11 | custom fusion | bytes 4210688 | tf_op jit(solution)/shard_map/gather | solution.py:80
  200.1 28.5 %all-to-all-done.7 = bf16[32,128,256]{2,1,0:T(8,128)(2,1)S(1)} async-done(((bf16[32,128,256]{2,1,0:T(8,128)(2,1)}), bf16[32,128,256]{2,1,0:T(8,128)(2,1)S(1)}, u32[]{:S(2)}, u32[]{:S(2)}) %all-to-all-start.7) | async-done | bytes 2097184 | tf_op jit(solution)/shard_map/all_to_all | solution.py:75
  237.5 17.4 %all-reduce.6.cloned.1.call-done = f32[256,256]{1,0:T(8,128)} async-done(((f32[256,256]{1,0:T(8,128)}), f32[256,256]{1,0:T(8,128)}) %all-reduce.6.cloned.1.call-update) | async-done | bytes 262160 | tf_op jit(solution)/shard_map/psum | solution.py:82
  258.5 4.7 %all-to-all-start = ((s32[4,8,1]{1,2,0:T(1,128)}), s32[4,8,1]{1,2,0:T(1,128)S(1)}, u32[]{:S(2)}, u32[]{:S(2)}) async-start(s32[4,8,1]{1,2,0:T(1,128)} %bitcast.3), calls=%async_computation | async-start | bytes 4096 | tf_op jit(solution)/shard_map/all_to_all | solution.py:77
  265.2 7.3 %reduce-scatter.6.cloned.1.call-done = f32[256,256]{1,0:T(8,128)} async-done(((f32[256,512]{1,0:T(8,128)}), f32[256,256]{1,0:T(8,128)}) %reduce-scatter.6.cloned.1.call-update) | async-done | bytes 262160 | tf_op jit(solution)/shard_map/reduce_scatter | solution.py:85
  273.5 5.0 %all_gather.17 = bf16[256,512]{1,0:T(8,128)(2,1)S(1)} all-gather(bf16[256,256]{1,0:T(8,128)(2,1)S(1)} %add_convert_fusion.1), channel_id=1, replica_groups=mesh['groups'=2,'space'=4,'feat'=2,'sub'=2] {'feat'}, dimensions={1}, use_global_device_ids=true | all-gather | bytes 393216 | tf_op jit(solution)/shard_map/all_gather | solution.py:42
  279.7 14.6 %gather_fusion.13 = bf16[4096,256]{1,0:T(8,128)(2,1)S(1)} fusion(bf16[256,256]{1,0:T(8,128)(2,1)S(1)} %convolution_convert_fusion.1, s32[4096]{0:T(1024)S(1)} %fusion.48), kind=kCustom, calls=%fused_computation.13 | custom fusion | bytes 4210688 | tf_op jit(solution)/shard_map/gather | solution.py:72
  294.3 4.5 %all-to-all-start.1 = ((s32[4,8,128]{2,1,0:T(8,128)}), s32[4,8,128]{2,1,0:T(8,128)S(1)}, u32[]{:S(2)}, u32[]{:S(2)}) async-start(s32[4,8,128]{2,1,0:T(8,128)} %bitcast_select_fusion.2), calls=%async_computation.1 | async-start | bytes 32768 | tf_op jit(solution)/shard_map/all_to_all | solution.py:76
  309.2 16.9 %gather_fusion.14 = bf16[4096,256]{1,0:T(8,128)(2,1)} fusion(bf16[256,256]{1,0:T(8,128)(2,1)S(1)} %convolution_convert_fusion, s32[4096]{0:T(1024)S(1)} %fusion.50), kind=kCustom, calls=%fused_computation.14 | custom fusion | bytes 4210688 | tf_op jit(solution)/shard_map/gather | solution.py:80
  326.1 28.4 %all-to-all-done.8 = bf16[32,128,256]{2,1,0:T(8,128)(2,1)S(1)} async-done(((bf16[32,128,256]{2,1,0:T(8,128)(2,1)}), bf16[32,128,256]{2,1,0:T(8,128)(2,1)S(1)}, u32[]{:S(2)}, u32[]{:S(2)}) %all-to-all-start.8) | async-done | bytes 2097184 | tf_op jit(solution)/shard_map/all_to_all | solution.py:75
  363.1 17.7 %all-reduce.8.cloned.1.call-done = f32[256,256]{1,0:T(8,128)} async-done(((f32[256,256]{1,0:T(8,128)}), f32[256,256]{1,0:T(8,128)}) %all-reduce.8.cloned.1.call-update) | async-done | bytes 262160 | tf_op jit(solution)/shard_map/psum | solution.py:82
  382.9 15.5 %reduce-scatter.8.cloned.1.call-done = f32[256,256]{1,0:T(8,128)} async-done(((f32[256,512]{1,0:T(8,128)}), f32[256,256]{1,0:T(8,128)}) %reduce-scatter.8.cloned.1.call-update) | async-done | bytes 262160 | tf_op jit(solution)/shard_map/reduce_scatter | solution.py:85
  (133 shorter events, 91.5 us)
Async XLA Ops:
  6.5 12.6 %copy-start = (bf16[256,227]{0,1:T(8,128)(2,1)S(1)}, bf16[256,227]{0,1:T(8,128)(2,1)}, u32[]{:S(2)}) copy-start(bf16[256,227]{0,1:T(8,128)(2,1)} %param.19) | copy-start | bytes 348676
  11.0 30.3 %all-to-all-start.2 = ((s32[4,8,1]{1,2,0:T(1,128)}), s32[4,8,1]{1,2,0:T(1,128)S(1)}, u32[]{:S(2)}, u32[]{:S(2)}) async-start(s32[4,8,1]{1,2,0:T(1,128)} %bitcast.10), calls=%async_computation.2 | async-start | bytes 4096 | tf_op jit(solution)/shard_map/all_to_all | solution.py:77
  41.3 9.0 %all-to-all-start.3 = ((s32[4,8,128]{2,1,0:T(8,128)}), s32[4,8,128]{2,1,0:T(8,128)S(1)}, u32[]{:S(2)}, u32[]{:S(2)}) async-start(s32[4,8,128]{2,1,0:T(8,128)} %bitcast_select_fusion.1), calls=%async_computation.3 | async-start | bytes 32768 | tf_op jit(solution)/shard_map/all_to_all | solution.py:76
  47.4 11.1 %copy-start.9 = (f32[3,256]{1,0:T(4,128)S(1)}, f32[3,256]{1,0:T(4,128)}, u32[]{:S(2)}) copy-start(f32[3,256]{1,0:T(4,128)} %param.25) | copy-start | bytes 9220
  50.3 51.3 %all-to-all-start.4 = ((bf16[32,128,256]{2,1,0:T(8,128)(2,1)}), bf16[32,128,256]{2,1,0:T(8,128)(2,1)S(1)}, u32[]{:S(2)}, u32[]{:S(2)}) async-start(bf16[32,128,256]{2,1,0:T(8,128)(2,1)} %broadcast_select_fusion.1), calls=%async_computation.4 | async-start | bytes 4194304 | tf_op jit(solution)/shard_map/all_to_all | solution.py:75
  53.9 74.9 %all-reduce.4.cloned.1.call-start = ((), (), s32[]{:S(2)}) async-start(), calls=%async_computation.12 | async-start | bytes 524288 | tf_op jit(solution)/shard_map/psum | solution.py:82
  109.3 21.8 %copy-start.1 = (s32[16]{0:T(128)S(1)}, s32[16]{0:T(128)}, u32[]{:S(2)}) copy-start(s32[16]{0:T(128)} %param.32) | copy-start | bytes 196
  109.3 28.0 %copy-start.3 = (s32[16,128]{1,0:T(8,128)S(1)}, s32[16,128]{1,0:T(8,128)}, u32[]{:S(2)}) copy-start(s32[16,128]{1,0:T(8,128)} %param.30) | copy-start | bytes 24580
  109.3 28.6 %copy-start.4 = (s32[16,128]{1,0:T(8,128)S(1)}, s32[16,128]{1,0:T(8,128)}, u32[]{:S(2)}) copy-start(s32[16,128]{1,0:T(8,128)} %param.33) | copy-start | bytes 24580
  110.1 36.4 %reduce-scatter.4.cloned.1.call-start = ((), (), s32[]{:S(2)}) async-start(), calls=%async_computation.13 | async-start | bytes 786432 | tf_op jit(solution)/shard_map/reduce_scatter | solution.py:85
  132.5 35.8 %all-to-all-start.5 = ((s32[4,8,1]{1,2,0:T(1,128)}), s32[4,8,1]{1,2,0:T(1,128)S(1)}, u32[]{:S(2)}, u32[]{:S(2)}) async-start(s32[4,8,1]{1,2,0:T(1,128)} %bitcast.28), calls=%async_computation.6 | async-start | bytes 4096 | tf_op jit(solution)/shard_map/all_to_all | solution.py:77
  168.3 9.0 %all-to-all-start.6 = ((s32[4,8,128]{2,1,0:T(8,128)}), s32[4,8,128]{2,1,0:T(8,128)S(1)}, u32[]{:S(2)}, u32[]{:S(2)}) async-start(s32[4,8,128]{2,1,0:T(8,128)} %bitcast_select_fusion), calls=%async_computation.7 | async-start | bytes 32768 | tf_op jit(solution)/shard_map/all_to_all | solution.py:76
  177.3 51.3 %all-to-all-start.7 = ((bf16[32,128,256]{2,1,0:T(8,128)(2,1)}), bf16[32,128,256]{2,1,0:T(8,128)(2,1)S(1)}, u32[]{:S(2)}, u32[]{:S(2)}) async-start(bf16[32,128,256]{2,1,0:T(8,128)(2,1)} %broadcast_select_fusion), calls=%async_computation.8 | async-start | bytes 4194304 | tf_op jit(solution)/shard_map/all_to_all | solution.py:75
  180.9 73.9 %all-reduce.6.cloned.1.call-start = ((), (), s32[]{:S(2)}) async-start(), calls=%async_computation.14 | async-start | bytes 524288 | tf_op jit(solution)/shard_map/psum | solution.py:82
  232.5 22.3 %copy-start.7 = (bf16[3,256,512]{2,1,0:T(8,128)(2,1)S(1)}, bf16[3,256,512]{2,1,0:T(8,128)(2,1)}, u32[]{:S(2)}) copy-start(bf16[3,256,512]{2,1,0:T(8,128)(2,1)} %param.24) | copy-start | bytes 2359300
  236.4 20.8 %copy-start.2 = (s32[16]{0:T(128)S(1)}, s32[16]{0:T(128)}, u32[]{:S(2)}) copy-start(s32[16]{0:T(128)} %param.36) | copy-start | bytes 196
  236.4 27.0 %copy-start.5 = (s32[16,128]{1,0:T(8,128)S(1)}, s32[16,128]{1,0:T(8,128)}, u32[]{:S(2)}) copy-start(s32[16,128]{1,0:T(8,128)} %param.34) | copy-start | bytes 24580
  236.4 27.6 %copy-start.6 = (s32[16,128]{1,0:T(8,128)S(1)}, s32[16,128]{1,0:T(8,128)}, u32[]{:S(2)}) copy-start(s32[16,128]{1,0:T(8,128)} %param.37) | copy-start | bytes 24580
  237.1 35.4 %reduce-scatter.6.cloned.1.call-start = ((), (), s32[]{:S(2)}) async-start(), calls=%async_computation.15 | async-start | bytes 786432 | tf_op jit(solution)/shard_map/reduce_scatter | solution.py:85
  258.5 35.8 %all-to-all-start = ((s32[4,8,1]{1,2,0:T(1,128)}), s32[4,8,1]{1,2,0:T(1,128)S(1)}, u32[]{:S(2)}, u32[]{:S(2)}) async-start(s32[4,8,1]{1,2,0:T(1,128)} %bitcast.3), calls=%async_computation | async-start | bytes 4096 | tf_op jit(solution)/shard_map/all_to_all | solution.py:77
  294.3 9.0 %all-to-all-start.1 = ((s32[4,8,128]{2,1,0:T(8,128)}), s32[4,8,128]{2,1,0:T(8,128)S(1)}, u32[]{:S(2)}, u32[]{:S(2)}) async-start(s32[4,8,128]{2,1,0:T(8,128)} %bitcast_select_fusion.2), calls=%async_computation.1 | async-start | bytes 32768 | tf_op jit(solution)/shard_map/all_to_all | solution.py:76
  303.3 51.3 %all-to-all-start.8 = ((bf16[32,128,256]{2,1,0:T(8,128)(2,1)}), bf16[32,128,256]{2,1,0:T(8,128)(2,1)S(1)}, u32[]{:S(2)}, u32[]{:S(2)}) async-start(bf16[32,128,256]{2,1,0:T(8,128)(2,1)} %broadcast_select_fusion.2), calls=%async_computation.10 | async-start | bytes 4194304 | tf_op jit(solution)/shard_map/all_to_all | solution.py:75
  306.9 73.9 %all-reduce.8.cloned.1.call-start = ((), (), s32[]{:S(2)}) async-start(), calls=%async_computation.16 | async-start | bytes 524288 | tf_op jit(solution)/shard_map/psum | solution.py:82
  363.1 35.4 %reduce-scatter.8.cloned.1.call-start = ((), (), s32[]{:S(2)}) async-start(), calls=%async_computation.17 | async-start | bytes 786432 | tf_op jit(solution)/shard_map/reduce_scatter | solution.py:85
  (3 other events, 15.9 us)
Sparse Core Ops, SparseCore 0:
  110.2 18.5 all-reduce.3
  131.1 15.3 reduce-scatter.3
  237.2 17.5 all-reduce.5
  257.1 15.3 reduce-scatter.5
  363.2 17.5 all-reduce.7
  383.1 15.3 reduce-scatter.7
where the time goes:
time: 409 us; the launch traced here: 407 us
  waiting for transfers between devices  173 us (42%)
  local copies, waits for them, and re-layouts  108 us (26%)
  starting transfers between devices  39.8 us (10%)
  matrix products  37.9 us (9%)
  blocking collectives  19 us (5%)
  other arithmetic  15.9 us (4%)
  between operations  13.8 us (3%)
    all_to_all x3, waiting for transfers between devices, section(): lax.all_to_all(sent_data, 'space', split_axis=0, concat_axis=0, tiled=True)  80.6 us
    psum x3, waiting for transfers between devices, section(): edge_sums = lax.psum(edge_sums, 'sub')  53.4 us
    gather x3, local copies, waits for them, and re-layouts, section(): recv_proj[target_rows]  50.8 us
    gather x6, local copies, waits for them, and re-layouts, section(): send_rows = send_proj[sources[block_pick]]  46.3 us
    reduce_scatter x3, waiting for transfers between devices, section(): lax.psum_scatter(partial_update, 'feat', scatter_dimension=1, tiled=True)  30.2 us
    all_to_all x3, starting transfers between devices, section(): lax.all_to_all(sent_blocks, 'space', split_axis=0, concat_axis=0, tiled=T...  14.8 us
    all_gather x3, blocking collectives, section(): lax.all_gather(sender, 'feat', axis=1, tiled=True)  14.5 us
    all_to_all x3, starting transfers between devices, section(): lax.all_to_all(sent_offsets, 'space', split_axis=0, concat_axis=0, tiled=...  13.5 us
  transfers between devices with their start and end apart: 15, of which 12 were waited for; matrix products, arithmetic and copies ran while one was open for 30% of the time, Pallas kernels for 0%

commit v1 on v0

--- a/solution.py
+++ b/solution.py
@@ -1,6 +1,10 @@
+import functools
+
 import jax
 import jax.numpy as jnp
 from jax import lax
+from jax.experimental import pallas as pl
+from jax.experimental.pallas import tpu as pltpu
 from jax.sharding import PartitionSpec as P
 
 
@@ -149,6 +153,412 @@
     )
 
 
+MESH = pl.DeviceIdType.MESH
+LANES = 128
+CAP = 8
+CHUNK = 4
+F32 = jnp.float32
+BF16 = jnp.bfloat16
+
+
+def fits_kernel(mesh):
+    sizes = mesh.shape
+    return sizes["feat"] == 2 and sizes["sub"] == 2 and sizes["space"] == 4
+
+
+def partner(me, k):
+    result, bit = me, 1
+    while bit <= k:
+        if k & bit:
+            result = result + bit - 2 * bit * lax.rem(lax.div(me, bit), 2)
+        bit *= 2
+    return result
+
+
+def mm(a, b):
+    return jnp.dot(a, b, preferred_element_type=F32)
+
+
+def fused_kernel(
+    n_space,
+    x_ref,
+    mesh_ref,
+    w_embed_ref,
+    w_send_ref,
+    w_recv_ref,
+    w_out_ref,
+    bias_ref,
+    small_ref,
+    small_row_ref,
+    src0_ref,
+    off0_ref,
+    src1_ref,
+    off1_ref,
+    src2_ref,
+    off2_ref,
+    out_ref,
+    grid_full,
+    mesh_full,
+    latent,
+    meta_send,
+    meta_buf,
+    ps_buf,
+    pr_buf,
+    agg_buf,
+    wout_peer,
+    wout_last,
+    bias_buf,
+    hots,
+    meta_ss,
+    meta_rs,
+    feat_ss,
+    feat_rs,
+    ps_ss,
+    ps_rs,
+    agg_ss,
+    agg_rs,
+):
+    s_me = lax.axis_index("space")
+    f_me = lax.axis_index("feat")
+    u_me = lax.axis_index("sub")
+    f_other, u_other = 1 - f_me, 1 - u_me
+    sends = []
+
+    def remote(src, dst, send_sem, recv_sem, space=None, feat=None, sub=None):
+        return pltpu.make_async_remote_copy(
+            src_ref=src,
+            dst_ref=dst,
+            send_sem=send_sem,
+            recv_sem=recv_sem,
+            device_id={
+                "space": s_me if space is None else space,
+                "feat": f_me if feat is None else feat,
+                "sub": u_me if sub is None else sub,
+            },
+            device_id_type=MESH,
+        )
+
+    def push(*args, **kwargs):
+        copy = remote(*args, **kwargs)
+        copy.start()
+        sends.append(copy)
+
+    meta_peers = [
+        (partner(s_me, k), u_other if flip else u_me)
+        for k in range(n_space)
+        for flip in (0, 1)
+        if k or flip
+    ]
+    quad_peers = [(f_me, u_other), (f_other, u_me), (f_other, u_other)]
+
+    barrier = pltpu.get_barrier_semaphore()
+    for space, sub in meta_peers:
+        pl.semaphore_signal(
+            barrier,
+            inc=1,
+            device_id={"space": space, "feat": f_me, "sub": sub},
+            device_id_type=MESH,
+        )
+    for feat, sub in quad_peers[1:]:
+        pl.semaphore_signal(
+            barrier,
+            inc=1,
+            device_id={"space": s_me, "feat": feat, "sub": sub},
+            device_id_type=MESH,
+        )
+
+    grid_full[f_me] = mm(x_ref[...], w_embed_ref[...]).astype(BF16)
+    mesh_full[f_me] = mesh_ref[...]
+
+    block_count = small_ref.shape[0]
+    slot_count = n_space * CAP
+    before = lax.broadcasted_iota(jnp.int32, (block_count, block_count), 0) < lax.broadcasted_iota(
+        jnp.int32, (block_count, block_count), 1
+    )
+    for t, (src_ref, off_ref) in enumerate(
+        ((src0_ref, off0_ref), (src1_ref, off1_ref), (src2_ref, off2_ref))
+    ):
+        own_col = small_ref[:, 2 * t : 2 * t + 1]
+        block_col = small_ref[:, 2 * t + 1 : 2 * t + 2]
+        own_row = small_row_ref[2 * t : 2 * t + 1, :]
+        earlier = jnp.where((own_col == own_row) & before, 1.0, 0.0)
+        rank = jnp.sum(earlier, axis=0, keepdims=True)
+        slot_row = own_row.astype(F32) * float(CAP) + rank
+        slots = lax.broadcasted_iota(jnp.int32, (slot_count, block_count), 0).astype(F32)
+        pick = jnp.where(slots == slot_row, 1.0, 0.0).astype(BF16)
+        offs = off_ref[...]
+        rows = jnp.where(offs >= 0, offs + 128 * block_col + 1, 0).astype(F32).astype(BF16)
+        src_slots = mm(pick, src_ref[...].astype(F32).astype(BF16))
+        row_slots = mm(pick, rows)
+        for o in range(n_space):
+            part = slice(o * CAP, (o + 1) * CAP)
+            meta_send[o, t] = jnp.concatenate([src_slots[part], row_slots[part]], axis=0).astype(
+                BF16
+            )
+    my_slot = s_me * 2 + u_me
+    meta_buf[my_slot] = meta_send[s_me]
+
+    pl.semaphore_wait(barrier, len(meta_peers) + 2)
+
+    def feat_copy(index, src, dst):
+        return remote(src, dst, feat_ss.at[index], feat_rs.at[index], feat=f_other)
+
+    def feat_push(index, src, dst):
+        copy = feat_copy(index, src, dst)
+        copy.start()
+        sends.append(copy)
+
+    feat_push(0, grid_full.at[f_me], grid_full.at[f_me])
+    for i, (space, sub) in enumerate(meta_peers):
+        push(
+            meta_send.at[space],
+            meta_buf.at[my_slot],
+            meta_ss.at[i],
+            meta_rs.at[my_slot],
+            space=space,
+            sub=sub,
+        )
+    feat_push(1, mesh_ref, mesh_full.at[f_me])
+    feat_push(2, w_out_ref.at[0], wout_peer.at[0])
+
+    hid_cols = pl.ds(pl.multiple_of(u_me * LANES, LANES), LANES)
+    for t in range(3):
+        row = bias_ref[t : t + 1, hid_cols]
+        bias_buf[t] = jnp.transpose(jnp.broadcast_to(row, (LANES, LANES)))
+
+    def project(latents, weight_ref, t):
+        width = latents.shape[2]
+        total = mm(latents[0], weight_ref[t, 0:width, hid_cols])
+        total += mm(latents[1], weight_ref[t, width : 2 * width, hid_cols])
+        return jnp.transpose(total).astype(BF16)
+
+    def start_ps(latents, t):
+        ps_buf[t, s_me] = project(latents, w_send_ref, t)
+        for k in range(1, n_space):
+            push(
+                ps_buf.at[t, s_me],
+                ps_buf.at[t, s_me],
+                ps_ss.at[t, k],
+                ps_rs.at[t, s_me],
+                space=partner(s_me, k),
+            )
+
+    rows_count = mesh_ref.shape[0]
+
+    def build_hots(t):
+        node = lax.broadcasted_iota(jnp.int32, (rows_count, LANES), 0).astype(F32)
+
+        def body(i, carry):
+            meta = meta_buf[i, t].astype(F32)
+            for j in range(CAP):
+                lanes = slice((j % CHUNK) * LANES, (j % CHUNK + 1) * LANES)
+                place = i * (CAP // CHUNK) + j // CHUNK
+                hots[t, place, 0:rows_count, lanes] = jnp.where(
+                    node == meta[j : j + 1], 1.0, 0.0
+                ).astype(BF16)
+                hots[t, place, rows_count : 2 * rows_count, lanes] = jnp.where(
+                    node + 1.0 == meta[CAP + j : CAP + j + 1], 1.0, 0.0
+                ).astype(BF16)
+            return carry
+
+        lax.fori_loop(0, 2 * n_space, body, 0)
+
+    def edges(t):
+        per_space = 2 * CAP // CHUNK
+        recv_table = pr_buf[t]
+        bias = jnp.concatenate([bias_buf[t]] * CHUNK, axis=1)
+        total = jnp.zeros((rows_count, LANES), F32)
+        for k in range(n_space):
+            space = partner(s_me, k)
+            if k:
+                remote(
+                    ps_buf.at[t, space],
+                    ps_buf.at[t, space],
+                    ps_ss.at[t, k],
+                    ps_rs.at[t, space],
+                    space=space,
+                ).wait_recv()
+            send_table = ps_buf[t, space]
+
+            def body(c, acc, send_table=send_table, space=space):
+                place = space * per_space + c
+                send_hot = hots[t, place, 0:rows_count, :]
+                recv_hot = hots[t, place, rows_count : 2 * rows_count, :]
+                half = 0.5 * (mm(send_table, send_hot) + mm(recv_table, recv_hot) + bias)
+                hidden = (half + half * jnp.tanh(half)).astype(BF16)
+                return acc + lax.dot_general(
+                    recv_hot, hidden, (((1,), (1,)), ((), ())), preferred_element_type=F32
+                )
+
+            total = lax.fori_loop(0, per_space, body, total)
+        return total
+
+    q_me = f_me * 2 + u_me
+
+    def start_agg(t, total):
+        agg_buf[t, q_me] = total.astype(BF16)
+        for i, (feat, sub) in enumerate(quad_peers):
+            push(
+                agg_buf.at[t, q_me],
+                agg_buf.at[t, q_me],
+                agg_ss.at[t, i],
+                agg_rs.at[t, q_me],
+                feat=feat,
+                sub=sub,
+            )
+
+    def wait_agg(t):
+        for i, (feat, sub) in enumerate(quad_peers):
+            q = feat * 2 + sub
+            remote(
+                agg_buf.at[t, q],
+                agg_buf.at[t, q],
+                agg_ss.at[t, i],
+                agg_rs.at[t, q],
+                feat=feat,
+                sub=sub,
+            ).wait_recv()
+        own = jnp.concatenate([agg_buf[t, f_me * 2], agg_buf[t, f_me * 2 + 1]], axis=1)
+        other = jnp.concatenate([agg_buf[t, f_other * 2], agg_buf[t, f_other * 2 + 1]], axis=1)
+        return own, other
+
+    def advance(base, t, to):
+        own, other = wait_agg(t)
+        feat_copy(2 + t, w_out_ref.at[t], wout_peer.at[t]).wait_recv()
+        width = base.shape[2]
+        for f in range(2):
+            cols = slice(f * width, (f + 1) * width)
+            update = mm(own, w_out_ref[t, :, cols]) + mm(other, wout_peer[t, :, cols])
+            latent[to, f] = (base[f].astype(F32) + update).astype(BF16)
+
+    for i, (space, sub) in enumerate(meta_peers):
+        slot = space * 2 + sub
+        remote(
+            meta_send.at[space],
+            meta_buf.at[slot],
+            meta_ss.at[i],
+            meta_rs.at[slot],
+            space=space,
+            sub=sub,
+        ).wait_recv()
+    feat_copy(0, grid_full.at[f_other], grid_full.at[f_other]).wait_recv()
+    start_ps(grid_full, 0)
+    build_hots(0)
+    feat_copy(1, mesh_ref, mesh_full.at[f_other]).wait_recv()
+    pr_buf[0] = project(mesh_full, w_recv_ref, 0)
+    start_agg(0, edges(0))
+    build_hots(1)
+    advance(mesh_full, 0, 0)
+
+    feat_push(3, w_out_ref.at[1], wout_peer.at[1])
+    start_ps(latent.at[0], 1)
+    pr_buf[1] = project(latent.at[0], w_recv_ref, 1)
+    pr_buf[2] = project(grid_full, w_recv_ref, 2)
+    start_agg(1, edges(1))
+    build_hots(2)
+    advance(latent.at[0], 1, 1)
+
+    half_width = out_ref.shape[1]
+    their_cols = pl.ds(pl.multiple_of(f_other * half_width, LANES), half_width)
+    my_cols = pl.ds(pl.multiple_of(f_me * half_width, LANES), half_width)
+    feat_push(4, w_out_ref.at[2, :, their_cols], wout_last)
+    start_ps(latent.at[1], 2)
+    start_agg(2, edges(2))
+    own, other = wait_agg(2)
+    feat_copy(4, w_out_ref.at[2, :, their_cols], wout_last).wait_recv()
+    update = mm(own, w_out_ref[2, :, my_cols]) + mm(other, wout_last[...])
+    out_ref[...] = (grid_full[f_me].astype(F32) + update).astype(BF16)
+    for copy in sends:
+        copy.wait_send()
+
+
+def fused_on_device(
+    n_space,
+    x_grid,
+    mesh_nodes,
+    w_embed,
+    w_send,
+    w_recv,
+    w_out,
+    edge_bias,
+    enc_sources,
+    enc_owners,
+    enc_blocks,
+    enc_offsets,
+    proc_sources,
+    proc_owners,
+    proc_blocks,
+    proc_offsets,
+    dec_sources,
+    dec_owners,
+    dec_blocks,
+    dec_offsets,
+):
+    small = jnp.concatenate(
+        [
+            enc_owners,
+            enc_blocks[:, None],
+            proc_owners,
+            proc_blocks[:, None],
+            dec_owners,
+            dec_blocks[:, None],
+        ],
+        axis=1,
+    )
+    rows, half = mesh_nodes.shape
+    lat = w_out.shape[2]
+    vmem = pl.BlockSpec(memory_space=pltpu.VMEM)
+    chunks = n_space * 2 * CAP // CHUNK
+    dma = pltpu.SemaphoreType.DMA
+    return pl.pallas_call(
+        functools.partial(fused_kernel, n_space),
+        out_shape=jax.ShapeDtypeStruct((rows, half), BF16),
+        in_specs=[vmem] * 15,
+        out_specs=vmem,
+        scratch_shapes=[
+            pltpu.VMEM((2, rows, half), BF16),
+            pltpu.VMEM((2, rows, half), BF16),
+            pltpu.VMEM((2, 2, rows, half), BF16),
+            pltpu.VMEM((n_space, 3, 2 * CAP, LANES), BF16),
+            pltpu.VMEM((2 * n_space, 3, 2 * CAP, LANES), BF16),
+            pltpu.VMEM((3, n_space, LANES, rows), BF16),
+            pltpu.VMEM((3, LANES, rows), BF16),
+            pltpu.VMEM((3, 4, rows, LANES), BF16),
+            pltpu.VMEM((2, half, lat), BF16),
+            pltpu.VMEM((half, half), BF16),
+            pltpu.VMEM((3, LANES, LANES), F32),
+            pltpu.VMEM((3, chunks, 2 * rows, CHUNK * LANES), BF16),
+            dma((2 * n_space,)),
+            dma((2 * n_space,)),
+            dma((5,)),
+            dma((5,)),
+            dma((3, n_space)),
+            dma((3, n_space)),
+            dma((3, 3)),
+            dma((3, 4)),
+        ],
+        compiler_params=pltpu.CompilerParams(
+            collective_id=0, has_side_effects=True, vmem_limit_bytes=52 * 1024 * 1024
+        ),
+    )(
+        x_grid,
+        mesh_nodes,
+        w_embed,
+        w_send,
+        w_recv,
+        w_out,
+        edge_bias,
+        small,
+        small.T,
+        enc_sources,
+        enc_offsets,
+        proc_sources,
+        proc_offsets,
+        dec_sources,
+        dec_offsets,
+    )
+
+
 def solution(mesh):
     in_specs = (
         P(("groups", "space"), None),
@@ -172,6 +582,9 @@
         P(("space", "sub"), None),
     )
     out_specs = P(("groups", "space"), "feat")
+    run = on_device
+    if fits_kernel(mesh):
+        run = functools.partial(fused_on_device, mesh.shape["space"])
     return jax.shard_map(
-        on_device, mesh=mesh, in_specs=in_specs, out_specs=out_specs, check_vma=False
-    )
+        run, mesh=mesh, in_specs=in_specs, out_specs=out_specs, check_vma=False
+    )

time: 409 us -> 63.5 us (0.16)
  waiting for transfers between devices: 173 us -> 0 us
  local copies, waits for them, and re-layouts: 108 us -> 7.07 us
  Pallas kernels: 0 us -> 55.9 us
  starting transfers between devices: 39.8 us -> 0 us
  matrix products: 37.9 us -> 0 us
  blocking collectives: 19 us -> 0 us
  other arithmetic: 15.9 us -> 0 us
  between operations: 13.8 us -> 0.11 us
    gather x15 -> x0, local copies, waits for them, and re-layouts: 102 us -> none  [the longest x3 50.8 us: section(): recv_proj[target_rows]]
    all_to_all x9 -> x0, waiting for transfers between devices: 89.4 us -> none  [the longest x3 80.6 us: section(): lax.all_to_all(sent_data, 'space', split_axis=0, concat_axis=0, tiled=True)]
    pallas_call x0 -> x1, Pallas kernels: none -> 55.9 us  [fused_on_device(): pl.pallas_call(functools.partial(fused_kernel, n_space), out_shape=jax.Sh...]
    psum x3 -> x0, waiting for transfers between devices: 53.4 us -> none  [section(): edge_sums = lax.psum(edge_sums, 'sub')]
    all_to_all x9 -> x0, starting transfers between devices: 39.1 us -> none  [the longest x3 14.8 us: section(): lax.all_to_all(sent_blocks, 'space', split_axis=0, concat_axis=0, tiled=T...]
    dot_general x16 -> x0, matrix products: 37.9 us -> none  [the longest x3 11.8 us: block_sum(): jnp.einsum('nep,nec->npc', node_hot, hidden, preferred_element_type=jnp.f...]
    reduce_scatter x3 -> x0, waiting for transfers between devices: 30.2 us -> none  [section(): lax.psum_scatter(partial_update, 'feat', scatter_dimension=1, tiled=True)]
    all_gather x4 -> x0, blocking collectives: 19 us -> none  [the longest x3 14.5 us: section(): lax.all_gather(sender, 'feat', axis=1, tiled=True)]
  transfers between devices with their start and end apart: 15 -> 0, of which waited for: 12 -> 0; matrix products, arithmetic and copies ran while one was open for 30% -> 0% of each run, Pallas kernels for 0% -> 0%
where the time goes in v1:
time: 63.5 us; the launch traced here: 63.1 us
  Pallas kernels  55.9 us (88%)
  local copies, waits for them, and re-layouts  7.07 us (11%)
    pallas_call x1, Pallas kernels, fused_on_device(): pl.pallas_call(functools.partial(fused_kernel, n_space), out_shape=jax.Sh...  55.9 us
    unnamed x32, local copies, waits for them, and re-layouts  6.3 us

profile of v1, /device:TPU:1, one launch (start us, length us, event | category | flops | bytes accessed | tf_op | source)
XLA Modules:
  0.0 63.1 jit_solution(13821985396404272640)
XLA Ops:
  0.0 0.0 copy-start.13
  0.0 0.0 copy-start.14
  0.0 0.0 copy-start.5
  0.0 0.6 copy-done.10
  0.7 0.0 copy-done.11
  0.7 0.0 copy-done.12
  0.7 0.0 copy-done.13
  0.7 0.0 copy-done.14
  0.7 0.7 %concatenate.3 = s32[16,6]{0,1:T(8,128)S(1)} concatenate(s32[16,1]{0,1:T(1,128)S(1)} %copy-done.10, s32[16,1]{0,1:T(1,128)S(1)} %bitcast.5, s32[16,1]{0,1:T(1,128)S(1)} %copy-done.12, s32[16,1]{0,1:T(1,128)S(1)} %bitcast.6, s32[16,1]{0,1:T(1,128)S(1)} %copy-done.14, s32[16,1]{0,1:T(1,128)} %bitcast.7), dimensions={1} | concatenate | bytes 768 | tf_op jit(solution)/shard_map/concatenate | solution.py:497
  1.4 0.1 copy.21.small_ref
  1.5 1.0 %copy.20.x_ref = bf16[256,227]{1,0:T(8,128)(2,1)S(1)} copy(bf16[256,227]{0,1:T(8,128)(2,1)} %param.19) | data formatting | bytes 232448 | tf_op args[0]
  2.5 0.0 copy-done.5
  2.6 0.0 copy-done.4
  2.6 0.0 copy-done.1
  2.6 0.0 copy-done.2
  2.6 0.0 copy-done.3
  2.6 0.0 copy-start
  2.6 1.1 %copy-done = bf16[3,512,256]{2,1,0:T(8,128)(2,1)S(1)} copy-done((bf16[3,512,256]{2,1,0:T(8,128)(2,1)S(1)}, bf16[3,512,256]{2,1,0:T(8,128)(2,1)}, u32[]{:S(2)}) %copy-start) | copy-done | bytes 786456
  3.7 0.7 %copy-done.6 = s32[16,128]{1,0:T(8,128)S(1)} copy-done((s32[16,128]{1,0:T(8,128)S(1)}, s32[16,128]{1,0:T(8,128)}, u32[]{:S(2)}) %copy-start.6) | copy-done | bytes 8216
  4.4 0.7 %copy-done.7 = s32[16,128]{1,0:T(8,128)S(1)} copy-done((s32[16,128]{1,0:T(8,128)S(1)}, s32[16,128]{1,0:T(8,128)}, u32[]{:S(2)}) %copy-start.7) | copy-done | bytes 8216
  5.1 0.7 %copy-done.8 = s32[16,128]{1,0:T(8,128)S(1)} copy-done((s32[16,128]{1,0:T(8,128)S(1)}, s32[16,128]{1,0:T(8,128)}, u32[]{:S(2)}) %copy-start.8) | copy-done | bytes 8216
  5.8 0.7 %copy-done.9 = f32[3,256]{1,0:T(4,128)S(1)} copy-done((f32[3,256]{1,0:T(4,128)S(1)}, f32[3,256]{1,0:T(4,128)}, u32[]{:S(2)}) %copy-start.9) | copy-done | bytes 3096
  6.5 55.9 %shard_map.181 = bf16[256,256]{1,0:T(8,128)(2,1)S(1)} custom-call(bf16[256,227]{1,0:T(8,128)(2,1)S(1)} %copy.20.x_ref, bf16[256,256]{1,0:T(8,128)(2,1)S(1)} %copy-done.1, bf16[227,256]{1,0:T(8,128)(2,1)S(1)} %copy-done.2, bf16[3,512,256]{2,1,0:T(8,128)(2,1)S(1)} %copy-done, bf16[3,512,256]{2,1,0:T(8,128)(2,1)} %w_recv_ref.1, bf16[3,256,512]{2,1,0:T(8,128)(2,1)} %w_out_ref.1, ...), custom_call_target="tpu_custom_call" | custom-call | tf_op jit(solution)/shard_map/pallas_call | solution.py:513
  62.4 0.7 %copy.23 = bf16[256,256]{1,0:T(8,128)(2,1)} copy(bf16[256,256]{1,0:T(8,128)(2,1)S(1)} %shard_map.181) | data formatting | bytes 262144
  (11 shorter events, 0.0 us)
Async XLA Ops:
  0.0 0.7 %copy-start.10 = (s32[16,1]{0,1:T(1,128)S(1)}, s32[16,1]{0,1:T(1,128)}, u32[]{:S(2)}) copy-start(s32[16,1]{0,1:T(1,128)} %param.27) | copy-start | bytes 196
  0.0 0.7 %copy-start.11 = (s32[16]{0:T(128)S(1)}, s32[16]{0:T(128)}, u32[]{:S(2)}) copy-start(s32[16]{0:T(128)} %param.28) | copy-start | bytes 196
  0.0 0.7 %copy-start.12 = (s32[16,1]{0,1:T(1,128)S(1)}, s32[16,1]{0,1:T(1,128)}, u32[]{:S(2)}) copy-start(s32[16,1]{0,1:T(1,128)} %param.31) | copy-start | bytes 196
  0.0 0.7 %copy-start.13 = (s32[16]{0:T(128)S(1)}, s32[16]{0:T(128)}, u32[]{:S(2)}) copy-start(s32[16]{0:T(128)} %param.32) | copy-start | bytes 196
  0.0 0.7 %copy-start.14 = (s32[16,1]{0,1:T(1,128)S(1)}, s32[16,1]{0,1:T(1,128)}, u32[]{:S(2)}) copy-start(s32[16,1]{0,1:T(1,128)} %param.35) | copy-start | bytes 196
  0.0 2.5 %copy-start.5 = (s32[16,128]{1,0:T(8,128)S(1)}, s32[16,128]{1,0:T(8,128)}, u32[]{:S(2)}) copy-start(s32[16,128]{1,0:T(8,128)} %src1_ref.1) | copy-start | bytes 24580
  0.7 1.8 %copy-start.4 = (s32[16,128]{1,0:T(8,128)S(1)}, s32[16,128]{1,0:T(8,128)}, u32[]{:S(2)}) copy-start(s32[16,128]{1,0:T(8,128)} %off0_ref.1) | copy-start | bytes 24580
  1.4 1.2 %copy-start.1 = (bf16[256,256]{1,0:T(8,128)(2,1)S(1)}, bf16[256,256]{1,0:T(8,128)(2,1)}, u32[]{:S(2)}) copy-start(bf16[256,256]{1,0:T(8,128)(2,1)} %mesh_ref.1) | copy-start | bytes 393220
  1.5 1.1 %copy-start.2 = (bf16[227,256]{1,0:T(8,128)(2,1)S(1)}, bf16[227,256]{1,0:T(8,128)(2,1)}, u32[]{:S(2)}) copy-start(bf16[227,256]{1,0:T(8,128)(2,1)} %w_embed_ref.1) | copy-start | bytes 348676
  1.5 1.1 %copy-start.3 = (s32[16,128]{1,0:T(8,128)S(1)}, s32[16,128]{1,0:T(8,128)}, u32[]{:S(2)}) copy-start(s32[16,128]{1,0:T(8,128)} %src0_ref.1) | copy-start | bytes 24580
  2.6 1.1 %copy-start = (bf16[3,512,256]{2,1,0:T(8,128)(2,1)S(1)}, bf16[3,512,256]{2,1,0:T(8,128)(2,1)}, u32[]{:S(2)}) copy-start(bf16[3,512,256]{2,1,0:T(8,128)(2,1)} %w_send_ref.1) | copy-start | bytes 2359300
  3.7 0.7 %copy-start.6 = (s32[16,128]{1,0:T(8,128)S(1)}, s32[16,128]{1,0:T(8,128)}, u32[]{:S(2)}) copy-start(s32[16,128]{1,0:T(8,128)} %off1_ref.1) | copy-start | bytes 24580
  4.4 0.7 %copy-start.7 = (s32[16,128]{1,0:T(8,128)S(1)}, s32[16,128]{1,0:T(8,128)}, u32[]{:S(2)}) copy-start(s32[16,128]{1,0:T(8,128)} %src2_ref.1) | copy-start | bytes 24580
  5.1 0.7 %copy-start.8 = (s32[16,128]{1,0:T(8,128)S(1)}, s32[16,128]{1,0:T(8,128)}, u32[]{:S(2)}) copy-start(s32[16,128]{1,0:T(8,128)} %off2_ref.1) | copy-start | bytes 24580
  5.8 0.7 %copy-start.9 = (f32[3,256]{1,0:T(4,128)S(1)}, f32[3,256]{1,0:T(4,128)}, u32[]{:S(2)}) copy-start(f32[3,256]{1,0:T(4,128)} %bias_ref.1) | copy-start | bytes 9220

commit v2 on v1

--- a/solution.py
+++ b/solution.py
@@ -181,22 +181,54 @@
 
 def fused_kernel(
     n_space,
+    x_hbm,
+    mesh_hbm,
+    w_embed_hbm,
+    w_send_hbm,
+    w_recv_hbm,
+    w_out_hbm,
+    bias_hbm,
+    *rest,
+):
+    edge_hbm, rest = rest[:12], rest[12:]
+    fused_body(
+        n_space,
+        x_hbm,
+        mesh_hbm,
+        w_embed_hbm,
+        w_send_hbm,
+        w_recv_hbm,
+        w_out_hbm,
+        bias_hbm,
+        edge_hbm,
+        *rest,
+    )
+
+
+def fused_body(
+    n_space,
+    x_hbm,
+    mesh_hbm,
+    w_embed_hbm,
+    w_send_hbm,
+    w_recv_hbm,
+    w_out_hbm,
+    bias_hbm,
+    edge_hbm,
+    out_ref,
     x_ref,
-    mesh_ref,
     w_embed_ref,
     w_send_ref,
     w_recv_ref,
     w_out_ref,
     bias_ref,
-    small_ref,
-    small_row_ref,
-    src0_ref,
-    off0_ref,
-    src1_ref,
-    off1_ref,
-    src2_ref,
-    off2_ref,
-    out_ref,
+    src_ref,
+    off_ref,
+    owner_ref,
+    block_ref,
+    fetch_sem,
+    sib_ss,
+    sib_rs,
     grid_full,
     mesh_full,
     latent,
@@ -223,6 +255,33 @@
     u_me = lax.axis_index("sub")
     f_other, u_other = 1 - f_me, 1 - u_me
     sends = []
+    fetched = {}
+    hid_cols = pl.ds(pl.multiple_of(u_me * LANES, LANES), LANES)
+    rows_count, half_width = mesh_hbm.shape
+    piece_rows = rows_count // 2
+    my_rows = pl.ds(pl.multiple_of(u_me * piece_rows, piece_rows), piece_rows)
+    sib_rows = pl.ds(pl.multiple_of(u_other * piece_rows, piece_rows), piece_rows)
+    wout_rows = half_width // 2
+    my_wout = pl.ds(pl.multiple_of(u_me * wout_rows, wout_rows), wout_rows)
+    sib_wout = pl.ds(pl.multiple_of(u_other * wout_rows, wout_rows), wout_rows)
+
+    def fetch(name, src, dst):
+        copy = pltpu.make_async_copy(src, dst, fetch_sem.at[len(fetched)])
+        copy.start()
+        fetched[name] = copy
+
+    fetch("x", x_hbm, x_ref)
+    fetch("w_embed", w_embed_hbm, w_embed_ref)
+    for t in range(3):
+        fetch(("owner", t), edge_hbm[4 * t], owner_ref.at[t])
+        fetch(("block", t), edge_hbm[4 * t + 1], block_ref.at[t])
+        fetch(("src", t), edge_hbm[4 * t + 2], src_ref.at[t])
+        fetch(("off", t), edge_hbm[4 * t + 3], off_ref.at[t])
+    fetch("mesh", mesh_hbm, mesh_full.at[f_me])
+    fetch("w_send", w_send_hbm.at[:, :, hid_cols], w_send_ref)
+    fetch("w_recv", w_recv_hbm.at[:, :, hid_cols], w_recv_ref)
+    fetch("bias", bias_hbm.at[:, hid_cols], bias_ref)
+    fetch("w_out", w_out_hbm, w_out_ref)
 
     def remote(src, dst, send_sem, recv_sem, space=None, feat=None, sub=None):
         return pltpu.make_async_remote_copy(
@@ -267,28 +326,37 @@
             device_id_type=MESH,
         )
 
-    grid_full[f_me] = mm(x_ref[...], w_embed_ref[...]).astype(BF16)
-    mesh_full[f_me] = mesh_ref[...]
-
-    block_count = small_ref.shape[0]
+    fetched["x"].wait()
+    fetched["w_embed"].wait()
+    grid_full[f_me] = lax.dot_general(
+        x_ref[...], w_embed_ref[...], (((0,), (0,)), ((), ())), preferred_element_type=F32
+    ).astype(BF16)
+
+    block_count = src_ref.shape[1]
     slot_count = n_space * CAP
-    before = lax.broadcasted_iota(jnp.int32, (block_count, block_count), 0) < lax.broadcasted_iota(
-        jnp.int32, (block_count, block_count), 1
-    )
-    for t, (src_ref, off_ref) in enumerate(
-        ((src0_ref, off0_ref), (src1_ref, off1_ref), (src2_ref, off2_ref))
-    ):
-        own_col = small_ref[:, 2 * t : 2 * t + 1]
-        block_col = small_ref[:, 2 * t + 1 : 2 * t + 2]
-        own_row = small_row_ref[2 * t : 2 * t + 1, :]
-        earlier = jnp.where((own_col == own_row) & before, 1.0, 0.0)
+    square = (block_count, block_count)
+    first = lax.broadcasted_iota(jnp.int32, square, 0)
+    second = lax.broadcasted_iota(jnp.int32, square, 1)
+    ones = jnp.ones((block_count, LANES), BF16)
+
+    def column(row):
+        spread = jnp.where(first == second, jnp.broadcast_to(row.astype(F32), square), 0.0)
+        return mm(spread.astype(BF16), ones)
+
+    for t in range(3):
+        for name in ("owner", "block", "src", "off"):
+            fetched[(name, t)].wait()
+        own_row = owner_ref[t]
+        own_col = column(own_row)[:, :block_count]
+        block_col = column(block_ref[t])
+        earlier = jnp.where((own_col == own_row.astype(F32)) & (first < second), 1.0, 0.0)
         rank = jnp.sum(earlier, axis=0, keepdims=True)
         slot_row = own_row.astype(F32) * float(CAP) + rank
         slots = lax.broadcasted_iota(jnp.int32, (slot_count, block_count), 0).astype(F32)
         pick = jnp.where(slots == slot_row, 1.0, 0.0).astype(BF16)
-        offs = off_ref[...]
-        rows = jnp.where(offs >= 0, offs + 128 * block_col + 1, 0).astype(F32).astype(BF16)
-        src_slots = mm(pick, src_ref[...].astype(F32).astype(BF16))
+        offs = off_ref[t].astype(F32)
+        rows = jnp.where(offs >= 0.0, offs + 128.0 * block_col + 1.0, 0.0).astype(BF16)
+        src_slots = mm(pick, src_ref[t].astype(F32).astype(BF16))
         row_slots = mm(pick, rows)
         for o in range(n_space):
             part = slice(o * CAP, (o + 1) * CAP)
@@ -308,7 +376,16 @@
         copy.start()
         sends.append(copy)
 
-    feat_push(0, grid_full.at[f_me], grid_full.at[f_me])
+    def sib_copy(index, ref):
+        return remote(ref, ref, sib_ss.at[index], sib_rs.at[index], sub=u_other)
+
+    def relay(index, arrived):
+        feat_copy(index, arrived, arrived).wait_recv()
+        copy = sib_copy(index, arrived)
+        copy.start()
+        sends.append(copy)
+
+    feat_push(0, grid_full.at[f_me, my_rows], grid_full.at[f_me, my_rows])
     for i, (space, sub) in enumerate(meta_peers):
         push(
             meta_send.at[space],
@@ -318,18 +395,18 @@
             space=space,
             sub=sub,
         )
-    feat_push(1, mesh_ref, mesh_full.at[f_me])
-    feat_push(2, w_out_ref.at[0], wout_peer.at[0])
-
-    hid_cols = pl.ds(pl.multiple_of(u_me * LANES, LANES), LANES)
+    feat_push(1, mesh_hbm.at[my_rows], mesh_full.at[f_me, my_rows])
+    feat_push(2, w_out_hbm.at[0, my_wout], wout_peer.at[0, my_wout])
+
+    fetched["bias"].wait()
     for t in range(3):
-        row = bias_ref[t : t + 1, hid_cols]
+        row = bias_ref[t : t + 1, :]
         bias_buf[t] = jnp.transpose(jnp.broadcast_to(row, (LANES, LANES)))
 
     def project(latents, weight_ref, t):
         width = latents.shape[2]
-        total = mm(latents[0], weight_ref[t, 0:width, hid_cols])
-        total += mm(latents[1], weight_ref[t, width : 2 * width, hid_cols])
+        total = mm(latents[0], weight_ref[t, 0:width, :])
+        total += mm(latents[1], weight_ref[t, width : 2 * width, :])
         return jnp.transpose(total).astype(BF16)
 
     def start_ps(latents, t):
@@ -342,8 +419,6 @@
                 ps_rs.at[t, s_me],
                 space=partner(s_me, k),
             )
-
-    rows_count = mesh_ref.shape[0]
 
     def build_hots(t):
         node = lax.broadcasted_iota(jnp.int32, (rows_count, LANES), 0).astype(F32)
@@ -390,7 +465,7 @@
                     recv_hot, hidden, (((1,), (1,)), ((), ())), preferred_element_type=F32
                 )
 
-            total = lax.fori_loop(0, per_space, body, total)
+            total = lax.fori_loop(0, per_space, body, total, unroll=True)
         return total
 
     q_me = f_me * 2 + u_me
@@ -424,7 +499,9 @@
 
     def advance(base, t, to):
         own, other = wait_agg(t)
-        feat_copy(2 + t, w_out_ref.at[t], wout_peer.at[t]).wait_recv()
+        sib_copy(2 + t, wout_peer.at[t, sib_wout]).wait_recv()
+        if t == 0:
+            fetched["w_out"].wait()
         width = base.shape[2]
         for f in range(2):
             cols = slice(f * width, (f + 1) * width)
@@ -441,31 +518,38 @@
             space=space,
             sub=sub,
         ).wait_recv()
-    feat_copy(0, grid_full.at[f_other], grid_full.at[f_other]).wait_recv()
+    relay(0, grid_full.at[f_other, my_rows])
+    fetched["w_send"].wait()
+    sib_copy(0, grid_full.at[f_other, sib_rows]).wait_recv()
     start_ps(grid_full, 0)
+    relay(1, mesh_full.at[f_other, my_rows])
     build_hots(0)
-    feat_copy(1, mesh_ref, mesh_full.at[f_other]).wait_recv()
+    fetched["w_recv"].wait()
+    fetched["mesh"].wait()
+    sib_copy(1, mesh_full.at[f_other, sib_rows]).wait_recv()
     pr_buf[0] = project(mesh_full, w_recv_ref, 0)
     start_agg(0, edges(0))
+    their_cols = pl.ds(pl.multiple_of(f_other * half_width, LANES), half_width)
+    my_cols = pl.ds(pl.multiple_of(f_me * half_width, LANES), half_width)
+    feat_push(3, w_out_hbm.at[1, my_wout], wout_peer.at[1, my_wout])
+    feat_push(4, w_out_hbm.at[2, my_wout, their_cols], wout_last.at[my_wout])
+    relay(2, wout_peer.at[0, my_wout])
     build_hots(1)
     advance(mesh_full, 0, 0)
 
-    feat_push(3, w_out_ref.at[1], wout_peer.at[1])
     start_ps(latent.at[0], 1)
     pr_buf[1] = project(latent.at[0], w_recv_ref, 1)
     pr_buf[2] = project(grid_full, w_recv_ref, 2)
     start_agg(1, edges(1))
+    relay(3, wout_peer.at[1, my_wout])
+    relay(4, wout_last.at[my_wout])
     build_hots(2)
     advance(latent.at[0], 1, 1)
 
-    half_width = out_ref.shape[1]
-    their_cols = pl.ds(pl.multiple_of(f_other * half_width, LANES), half_width)
-    my_cols = pl.ds(pl.multiple_of(f_me * half_width, LANES), half_width)
-    feat_push(4, w_out_ref.at[2, :, their_cols], wout_last)
     start_ps(latent.at[1], 2)
     start_agg(2, edges(2))
     own, other = wait_agg(2)
-    feat_copy(4, w_out_ref.at[2, :, their_cols], wout_last).wait_recv()
+    sib_copy(4, wout_last.at[sib_wout]).wait_recv()
     update = mm(own, w_out_ref[2, :, my_cols]) + mm(other, wout_last[...])
     out_ref[...] = (grid_full[f_me].astype(F32) + update).astype(BF16)
     for copy in sends:
@@ -494,28 +578,31 @@
     dec_blocks,
     dec_offsets,
 ):
-    small = jnp.concatenate(
-        [
-            enc_owners,
-            enc_blocks[:, None],
-            proc_owners,
-            proc_blocks[:, None],
-            dec_owners,
-            dec_blocks[:, None],
-        ],
-        axis=1,
-    )
     rows, half = mesh_nodes.shape
     lat = w_out.shape[2]
-    vmem = pl.BlockSpec(memory_space=pltpu.VMEM)
+    blocks = enc_sources.shape[0]
+    hbm = pl.BlockSpec(memory_space=pl.ANY)
     chunks = n_space * 2 * CAP // CHUNK
     dma = pltpu.SemaphoreType.DMA
     return pl.pallas_call(
         functools.partial(fused_kernel, n_space),
         out_shape=jax.ShapeDtypeStruct((rows, half), BF16),
-        in_specs=[vmem] * 15,
-        out_specs=vmem,
+        in_specs=[hbm] * 19,
+        out_specs=pl.BlockSpec(memory_space=pltpu.VMEM),
         scratch_shapes=[
+            pltpu.VMEM((x_grid.shape[1], rows), BF16),
+            pltpu.VMEM(w_embed.shape, BF16),
+            pltpu.VMEM((3, lat, LANES), BF16),
+            pltpu.VMEM((3, lat, LANES), BF16),
+            pltpu.VMEM(w_out.shape, BF16),
+            pltpu.VMEM((3, LANES), F32),
+            pltpu.VMEM((3, blocks, LANES), jnp.int32),
+            pltpu.VMEM((3, blocks, LANES), jnp.int32),
+            pltpu.VMEM((3, 1, blocks), jnp.int32),
+            pltpu.VMEM((3, 1, blocks), jnp.int32),
+            dma((19,)),
+            dma((5,)),
+            dma((5,)),
             pltpu.VMEM((2, rows, half), BF16),
             pltpu.VMEM((2, rows, half), BF16),
             pltpu.VMEM((2, 2, rows, half), BF16),
@@ -541,19 +628,23 @@
             collective_id=0, has_side_effects=True, vmem_limit_bytes=52 * 1024 * 1024
         ),
     )(
-        x_grid,
+        x_grid.T,
         mesh_nodes,
         w_embed,
         w_send,
         w_recv,
         w_out,
         edge_bias,
-        small,
-        small.T,
+        enc_owners.reshape(1, blocks),
+        enc_blocks.reshape(1, blocks),
         enc_sources,
         enc_offsets,
+        proc_owners.reshape(1, blocks),
+        proc_blocks.reshape(1, blocks),
         proc_sources,
         proc_offsets,
+        dec_owners.reshape(1, blocks),
+        dec_blocks.reshape(1, blocks),
         dec_sources,
         dec_offsets,
     )

time: 63.5 us -> 63.8 us (level)
  local copies, waits for them, and re-layouts: 7.07 us -> 11.3 us
  Pallas kernels: 55.9 us -> 52 us
    unnamed x32 -> x35, local copies, waits for them, and re-layouts: 6.3 us -> 11.3 us
    pallas_call x1, Pallas kernels: 55.9 us -> 52 us  [fused_on_device(): pl.pallas_call(functools.partial(fused_kernel, n_space), out_shape=jax.Sh...]
    concatenate x2 -> x0, local copies, waits for them, and re-layouts: 0.77 us -> none  [fused_on_device(): jnp.concatenate([enc_owners, enc_blocks[:, None], proc_owners, proc_block...]
where the time goes in v2:
time: 63.8 us; the launch traced here: 63.3 us
  Pallas kernels  52 us (82%)
  local copies, waits for them, and re-layouts  11.3 us (18%)
    pallas_call x1, Pallas kernels, fused_on_device(): pl.pallas_call(functools.partial(fused_kernel, n_space), out_shape=jax.Sh...  52 us
    unnamed x35, local copies, waits for them, and re-layouts  11.3 us

profile of v2, /device:TPU:1, one launch (start us, length us, event | category | flops | bytes accessed | tf_op | source)
XLA Modules:
  0.0 63.3 jit_solution(13121910343292900000)
XLA Ops:
  0.0 0.0 copy-start.4
  0.0 0.0 copy-start.10
  0.0 0.0 copy-start.11
  0.0 0.0 copy-start.12
  0.0 0.7 %copy-done.4 = s32[16,128]{1,0:T(8,128)S(1)} copy-done((s32[16,128]{1,0:T(8,128)S(1)}, s32[16,128]{1,0:T(8,128)}, u32[]{:S(2)}) %copy-start.4) | copy-done | bytes 8216
  0.7 0.0 copy-done.10
  0.7 0.0 copy-done.11
  0.7 0.0 copy-done.12
  0.7 0.0 copy-start
  0.7 1.1 %copy-done = bf16[3,512,256]{2,1,0:T(8,128)(2,1)S(1)} copy-done((bf16[3,512,256]{2,1,0:T(8,128)(2,1)S(1)}, bf16[3,512,256]{2,1,0:T(8,128)(2,1)}, u32[]{:S(2)}) %copy-start) | copy-done | bytes 786456
  1.8 0.9 %copy-done.1 = bf16[256,256]{1,0:T(8,128)(2,1)S(1)} copy-done((bf16[256,256]{1,0:T(8,128)(2,1)S(1)}, bf16[256,256]{1,0:T(8,128)(2,1)}, u32[]{:S(2)}) %copy-start.1) | copy-done | bytes 131096
  2.8 0.9 %copy-done.2 = bf16[256,227]{0,1:T(8,128)(2,1)S(1)} copy-done((bf16[256,227]{0,1:T(8,128)(2,1)S(1)}, bf16[256,227]{0,1:T(8,128)(2,1)}, u32[]{:S(2)}) %copy-start.2) | copy-done | bytes 116248
  3.7 0.9 %copy-done.3 = bf16[227,256]{1,0:T(8,128)(2,1)S(1)} copy-done((bf16[227,256]{1,0:T(8,128)(2,1)S(1)}, bf16[227,256]{1,0:T(8,128)(2,1)}, u32[]{:S(2)}) %copy-start.3) | copy-done | bytes 116248
  4.6 0.7 %copy-done.5 = s32[16,128]{1,0:T(8,128)S(1)} copy-done((s32[16,128]{1,0:T(8,128)S(1)}, s32[16,128]{1,0:T(8,128)}, u32[]{:S(2)}) %copy-start.5) | copy-done | bytes 8216
  5.2 0.7 %copy-done.6 = s32[16,128]{1,0:T(8,128)S(1)} copy-done((s32[16,128]{1,0:T(8,128)S(1)}, s32[16,128]{1,0:T(8,128)}, u32[]{:S(2)}) %copy-start.6) | copy-done | bytes 8216
  5.9 0.7 %copy-done.7 = s32[16,128]{1,0:T(8,128)S(1)} copy-done((s32[16,128]{1,0:T(8,128)S(1)}, s32[16,128]{1,0:T(8,128)}, u32[]{:S(2)}) %copy-start.7) | copy-done | bytes 8216
  6.6 0.7 %copy-done.8 = s32[16,128]{1,0:T(8,128)S(1)} copy-done((s32[16,128]{1,0:T(8,128)S(1)}, s32[16,128]{1,0:T(8,128)}, u32[]{:S(2)}) %copy-start.8) | copy-done | bytes 8216
  7.3 0.7 %copy-done.9 = s32[16,128]{1,0:T(8,128)S(1)} copy-done((s32[16,128]{1,0:T(8,128)S(1)}, s32[16,128]{1,0:T(8,128)}, u32[]{:S(2)}) %copy-start.9) | copy-done | bytes 8216
  8.0 0.7 %copy-done.13 = s32[16,1]{0,1:T(1,128)S(1)} copy-done((s32[16,1]{0,1:T(1,128)S(1)}, s32[16,1]{0,1:T(1,128)}, u32[]{:S(2)}) %copy-start.13) | copy-done | bytes 88
  8.7 0.7 %copy-done.14 = s32[16]{0:T(128)S(1)} copy-done((s32[16]{0:T(128)S(1)}, s32[16]{0:T(128)}, u32[]{:S(2)}) %copy-start.14) | copy-done | bytes 88
  9.3 0.7 %copy-done.15 = s32[16,1]{0,1:T(1,128)S(1)} copy-done((s32[16,1]{0,1:T(1,128)S(1)}, s32[16,1]{0,1:T(1,128)}, u32[]{:S(2)}) %copy-start.15) | copy-done | bytes 88
  10.0 0.7 %copy-done.16 = s32[16]{0:T(128)S(1)} copy-done((s32[16]{0:T(128)S(1)}, s32[16]{0:T(128)}, u32[]{:S(2)}) %copy-start.16) | copy-done | bytes 88
  10.7 52.0 %shard_map.181 = bf16[256,256]{1,0:T(8,128)(2,1)S(1)} custom-call(bf16[227,256]{1,0:T(8,128)(2,1)S(1)} %bitcast.7, bf16[256,256]{1,0:T(8,128)(2,1)S(1)} %copy-done.1, bf16[227,256]{1,0:T(8,128)(2,1)S(1)} %copy-done.3, bf16[3,512,256]{2,1,0:T(8,128)(2,1)S(1)} %copy-done, bf16[3,512,256]{2,1,0:T(8,128)(2,1)} %w_recv_hbm.1, bf16[3,256,512]{2,1,0:T(8,128)(2,1)} %w_out_hbm.1, ...), custom_call_target="tpu_custom_call" | custom-call | tf_op jit(solution)/shard_map/pallas_call | solution.py:587
  62.6 0.7 %copy.21 = bf16[256,256]{1,0:T(8,128)(2,1)} copy(bf16[256,256]{1,0:T(8,128)(2,1)S(1)} %shard_map.181) | data formatting | bytes 262144
  (12 shorter events, 0.0 us)
Async XLA Ops:
  0.0 0.7 %copy-start.4 = (s32[16,128]{1,0:T(8,128)S(1)}, s32[16,128]{1,0:T(8,128)}, u32[]{:S(2)}) copy-start(s32[16,128]{1,0:T(8,128)} %rest_2_.1) | copy-start | bytes 24580
  0.0 0.7 %copy-start.10 = (f32[3,256]{1,0:T(4,128)S(1)}, f32[3,256]{1,0:T(4,128)}, u32[]{:S(2)}) copy-start(f32[3,256]{1,0:T(4,128)} %bias_hbm.1) | copy-start | bytes 9220
  0.0 0.7 %copy-start.11 = (s32[16,1]{0,1:T(1,128)S(1)}, s32[16,1]{0,1:T(1,128)}, u32[]{:S(2)}) copy-start(s32[16,1]{0,1:T(1,128)} %param.27) | copy-start | bytes 196
  0.0 0.7 %copy-start.12 = (s32[16]{0:T(128)S(1)}, s32[16]{0:T(128)}, u32[]{:S(2)}) copy-start(s32[16]{0:T(128)} %param.28) | copy-start | bytes 196
  0.7 1.1 %copy-start = (bf16[3,512,256]{2,1,0:T(8,128)(2,1)S(1)}, bf16[3,512,256]{2,1,0:T(8,128)(2,1)}, u32[]{:S(2)}) copy-start(bf16[3,512,256]{2,1,0:T(8,128)(2,1)} %w_send_hbm.1) | copy-start | bytes 2359300
  1.8 0.9 %copy-start.1 = (bf16[256,256]{1,0:T(8,128)(2,1)S(1)}, bf16[256,256]{1,0:T(8,128)(2,1)}, u32[]{:S(2)}) copy-start(bf16[256,256]{1,0:T(8,128)(2,1)} %mesh_hbm.1) | copy-start | bytes 393220
  2.7 0.9 %copy-start.2 = (bf16[256,227]{0,1:T(8,128)(2,1)S(1)}, bf16[256,227]{0,1:T(8,128)(2,1)}, u32[]{:S(2)}) copy-start(bf16[256,227]{0,1:T(8,128)(2,1)} %param.19) | copy-start | bytes 348676
  3.6 0.9 %copy-start.3 = (bf16[227,256]{1,0:T(8,128)(2,1)S(1)}, bf16[227,256]{1,0:T(8,128)(2,1)}, u32[]{:S(2)}) copy-start(bf16[227,256]{1,0:T(8,128)(2,1)} %w_embed_hbm.1) | copy-start | bytes 348676
  4.5 0.7 %copy-start.5 = (s32[16,128]{1,0:T(8,128)S(1)}, s32[16,128]{1,0:T(8,128)}, u32[]{:S(2)}) copy-start(s32[16,128]{1,0:T(8,128)} %rest_3_.1) | copy-start | bytes 24580
  5.2 0.7 %copy-start.6 = (s32[16,128]{1,0:T(8,128)S(1)}, s32[16,128]{1,0:T(8,128)}, u32[]{:S(2)}) copy-start(s32[16,128]{1,0:T(8,128)} %rest_6_.1) | copy-start | bytes 24580
  5.9 0.7 %copy-start.7 = (s32[16,128]{1,0:T(8,128)S(1)}, s32[16,128]{1,0:T(8,128)}, u32[]{:S(2)}) copy-start(s32[16,128]{1,0:T(8,128)} %rest_7_.1) | copy-start | bytes 24580
  6.6 0.7 %copy-start.8 = (s32[16,128]{1,0:T(8,128)S(1)}, s32[16,128]{1,0:T(8,128)}, u32[]{:S(2)}) copy-start(s32[16,128]{1,0:T(8,128)} %rest_10_.1) | copy-start | bytes 24580
  7.3 0.7 %copy-start.9 = (s32[16,128]{1,0:T(8,128)S(1)}, s32[16,128]{1,0:T(8,128)}, u32[]{:S(2)}) copy-start(s32[16,128]{1,0:T(8,128)} %rest_11_.1) | copy-start | bytes 24580
  8.0 0.7 %copy-start.13 = (s32[16,1]{0,1:T(1,128)S(1)}, s32[16,1]{0,1:T(1,128)}, u32[]{:S(2)}) copy-start(s32[16,1]{0,1:T(1,128)} %param.31) | copy-start | bytes 196
  8.7 0.7 %copy-start.14 = (s32[16]{0:T(128)S(1)}, s32[16]{0:T(128)}, u32[]{:S(2)}) copy-start(s32[16]{0:T(128)} %param.32) | copy-start | bytes 196
  9.3 0.7 %copy-start.15 = (s32[16,1]{0,1:T(1,128)S(1)}, s32[16,1]{0,1:T(1,128)}, u32[]{:S(2)}) copy-start(s32[16,1]{0,1:T(1,128)} %param.35) | copy-start | bytes 196
  10.0 0.7 %copy-start.16 = (s32[16]{0:T(128)S(1)}, s32[16]{0:T(128)}, u32[]{:S(2)}) copy-start(s32[16]{0:T(128)} %param.36) | copy-start | bytes 196
